TPU v7x, 128 devices: a whole 4x4x4 slice. The times are simulated.
128 devices in a mesh: row: 16 (over x_lo, y, core), col: 8 (over z, x_hi).
Axes of the slice: x: 4 (x_hi: 2, x_lo: 2; x = x_hi * 2 + x_lo), y: 4, z: 4, core: 2. Of those that a mesh axis runs over, the one named last changes fastest.
Arguments:
- residual: float32 [16, 2048, 128], P(None, 'row'), may hold values from -6 to 6
- diag_inverse: bfloat16 [2, 2048, 2048], P(None, 'col', 'row'), as said below
- panels: bfloat16 [2, 16, 2048, 2048], P(None, None, 'row', 'col'), may hold values from -0.125 to 0.125
- first_block: int32 [1], replicated, may hold values from 0 to 14
- probe_solved: bfloat16 [16, 2048, 128], P(None, 'row'), may hold values from -6 to 6
- genotypes: bfloat16 [16, 2048, 16384], P(None, 'row', 'col'), may hold values from -6 to 6
- annotation: int32 [16384], P('col'), may hold values from 0 to 7
Outputs:
- trailing: float32 [16, 2048, 128], P(None, 'row')
- solved: float32 [2, 2048, 128], P(None, 'col')
- grm_products: bfloat16 [16, 2048, 8, 128], P(None, 'row', 'col')
Inputs may be any that keep to these rules, and one draw needn't show every extreme that they name: The two solve steps are blocks first_block and first_block + 1. diag_inverse is lower triangular in each of its two blocks.
All inputs are finite; a program needn't handle non-finite values.
Results may differ from a plain program's by a relative error of at most 0.0085.
Values may be sent and summed in bfloat16 or wider, within the bound.
A program may use at most 128 MiB of HBM per device.

v0:
```python
import jax
import jax.numpy as jnp
from jax import lax
from jax.sharding import PartitionSpec as P

A = 8
SNPS = 16384


def solve_panel(row_values, inverse_part):
    partial_value = jnp.dot(
        inverse_part, row_values.astype(jnp.bfloat16), preferred_element_type=jnp.float32
    )
    return lax.psum(partial_value, "row")


def panel_term(panel_part, solved_bf):
    return jnp.einsum("ngc,cr->ngr", panel_part, solved_bf, preferred_element_type=jnp.float32)


def shards(residual, diag_inverse, panels, first_block, probe_solved, genotypes, annotation):
    count_blocks = residual.shape[0]
    block_now = first_block[0]
    positions = jnp.arange(count_blocks, dtype=jnp.int32)
    current = residual
    solved_list = []
    for section in range(2):
        target = block_now + section
        row_values = lax.dynamic_index_in_dim(current, target, 0, keepdims=False)
        solved_now = solve_panel(row_values, diag_inverse[section])
        summed = lax.psum(panel_term(panels[section], solved_now.astype(jnp.bfloat16)), "col")
        keep_mask = (positions > target).astype(jnp.float32)[:, None, None]
        current = current - keep_mask * summed
        solved_list.append(solved_now)
    projected = jnp.einsum(
        "ngs,ngr->sr", genotypes, probe_solved, preferred_element_type=jnp.float32
    )
    inv_snps = 1.0 / SNPS
    loadings = lax.psum(projected, "row")
    rounded = (loadings * inv_snps).astype(jnp.bfloat16)
    onehot = annotation[:, None] == jnp.arange(A, dtype=jnp.int32)[None, :]
    weights = jnp.where(onehot[:, :, None], rounded[:, None, :], jnp.zeros((), jnp.bfloat16))
    weights = weights.reshape(rounded.shape[0], A * rounded.shape[1])
    annotated = jnp.einsum("ngs,sk->ngk", genotypes, weights, preferred_element_type=jnp.float32)
    annotated = annotated.reshape(genotypes.shape[0], genotypes.shape[1], A, rounded.shape[1])
    grm_products = lax.psum_scatter(annotated, "col", scatter_dimension=2, tiled=True).astype(
        jnp.bfloat16
    )
    return (current, jnp.stack(solved_list), grm_products)


def solution(mesh):
    in_specs = (
        P(None, "row", None),
        P(None, "col", "row"),
        P(None, None, "row", "col"),
        P(),
        P(None, "row", None),
        P(None, "row", "col"),
        P("col"),
    )
    out_specs = (P(None, "row", None), P(None, "col", None), P(None, "row", "col", None))
    return jax.shard_map(shards, mesh=mesh, in_specs=in_specs, out_specs=out_specs, check_vma=False)
```

profile of v0, /device:TPU:0, one launch (start us, length us, event | category | flops | bytes accessed | tf_op | source)
XLA Modules:
  0.0 740.2 jit_solution(16574658958006446606)
XLA Ops:
  7.2 0.0 copy-start
  7.2 0.0 copy-start.1
  7.2 0.0 all-reduce.8.cloned.1.call-start
  8.0 1.7 convolution_bitcast_fusion.4
  9.7 0.0 all-reduce.8.cloned.1.call-update
  9.7 0.0 all-reduce.10.cloned.1.call-start
  9.8 119.0 %all-reduce.8.cloned.1.call-done = f32[256,128]{0,1:T(8,128)} async-done(((f32[256,128]{0,1:T(8,128)}), f32[256,128]{0,1:T(8,128)}) %all-reduce.8.cloned.1.call-update) | async-done | bytes 131088 | tf_op jit(solution)/shard_map/psum | solution.py:14
  128.8 2.8 convolution_bitcast_fusion.2
  131.6 0.0 all-reduce.10.cloned.1.call-update
  131.6 0.0 all-reduce.14.cloned.1.call-start
  131.7 0.0 copy-done.1
  131.7 0.3 copy.16
  132.0 0.0 copy-done
  132.0 0.0 copy-start.4
  132.1 6.8 convolution_bitcast_fusion
  138.9 0.0 copy-start.6
  138.9 0.0 copy-start.5
  138.9 85.3 %all-reduce.10.cloned.1.call-done = f32[16,128,128]{1,2,0:T(8,128)} async-done(((f32[16,128,128]{1,2,0:T(8,128)}), f32[16,128,128]{1,2,0:T(8,128)}) %all-reduce.10.cloned.1.call-update) | async-done | bytes 1048592 | tf_op jit(solution)/shard_map/psum | solution.py:31
  224.2 1.4 multiply_subtract_fusion.1
  225.6 0.0 copy-done.4
  225.6 0.8 convolution_bitcast_fusion.3
  226.4 0.0 all-reduce.14.cloned.1.call-update
  226.5 0.0 all-reduce.12.cloned.1.call-start
  226.5 0.0 copy-done.6
  226.5 0.6 dynamic-slice
  227.1 0.0 copy-done.5
  227.1 118.4 %all-reduce.14.cloned.1.call-done = (f32[256,128]{0,1:T(8,128)}, f32[2048,128]{1,0:T(8,128)}) async-done(((f32[256,128]{0,1:T(8,128)}, f32[2048,128]{1,0:T(8,128)}), (f32[256,128]{0,1:T(8,128)}, f32[2048,128]{1,0:T(8,128)})) %all-reduce.14.cloned.1.call-update) | async-done | bytes 1179664 | tf_op jit(solution)/shard_map/psum | solution.py:14
  345.6 2.8 convolution_bitcast_fusion.1
  348.3 0.0 all-reduce.12.cloned.1.call-update
  348.3 1.3 multiply_convert_fusion
  349.6 0.2 copy.18
  349.8 0.4 broadcast_select_fusion
  350.2 12.4 %fusion.18 = f32[1024,16,128]{2,0,1:T(8,128)} fusion(bf16[2048,1024,1]{0,1,2:T(8,128)(2,1)S(1)} %bitcast.63, bf16[16,128,2048]{2,1,0:T(8,128)(2,1)} %param.12), kind=kOutput, calls=%fused_computation.32 | convolution fusion | flops 8589934592 | bytes 20971520 | tf_op jit(solution)/shard_map/ngs,sk->ngk/dot_general | solution.py:44
  362.6 9.3 %copy.19 = f32[16,128,8,128]{3,1,2,0:T(8,128)} copy(f32[16,128,8,128]{1,3,2,0:T(8,128)} %bitcast.62) | data formatting | bytes 16777216 | tf_op jit(solution)/shard_map/reshape | solution.py:45
  371.9 0.0 copy-start.2
  371.9 0.0 copy-start.3
  371.9 355.7 %all-reduce.15 = bf16[16,128,8,128]{3,1,2,0:T(8,128)(2,1)} all-reduce(f32[16,128,8,128]{3,1,2,0:T(8,128)} %copy.19), channel_id=2, replica_groups=mesh['row'=16,'col'=8] {'col'}, use_global_device_ids=true, to_apply=%region_5.6.clone | all-reduce | flops 2097152 | bytes 12582912
  727.6 0.0 copy-done.2
  727.6 0.0 copy-done.3
  727.6 0.8 copy.21
  728.5 2.4 dynamic-slice_convert_fusion
  730.9 0.0 all-reduce.12.cloned.1.call-done
  730.9 1.4 multiply_subtract_fusion
  732.3 1.3 copy.20
  (4 shorter events, 0.0 us)
Async XLA Ops:
  7.2 124.9 %copy-start = (bf16[16,128,128]{2,1,0:T(8,128)(2,1)S(1)}, bf16[16,128,128]{2,1,0:T(8,128)(2,1)}, u32[]{:S(2)}) copy-start(bf16[16,128,128]{2,1,0:T(8,128)(2,1)} %param.11) | copy-start | bytes 1572868
  7.2 124.5 %copy-start.1 = (f32[16,128,128]{2,1,0:T(8,128)S(1)}, f32[16,128,128]{2,1,0:T(8,128)}, u32[]{:S(2)}) copy-start(f32[16,128,128]{2,1,0:T(8,128)} %param.7) | copy-start | bytes 3145732
  7.2 121.7 %all-reduce.8.cloned.1.call-start = ((), (), s32[]{:S(2)}) async-start(), calls=%async_computation | async-start | bytes 262144 | tf_op jit(solution)/shard_map/psum | solution.py:14
  9.7 214.5 %all-reduce.10.cloned.1.call-start = ((), (), s32[]{:S(2)}) async-start(), calls=%async_computation.1 | async-start | bytes 2097152 | tf_op jit(solution)/shard_map/psum | solution.py:31
  131.6 213.9 %all-reduce.14.cloned.1.call-start = ((), (), s32[]{:S(2)}) async-start(), calls=%async_computation.3 | async-start | bytes 2359296 | tf_op jit(solution)/shard_map/psum | solution.py:14
  132.0 93.6 %copy-start.4 = (bf16[2,256,128]{2,1,0:T(8,128)(2,1)S(1)}, bf16[2,256,128]{2,1,0:T(8,128)(2,1)}, u32[]{:S(2)}) copy-start(bf16[2,256,128]{2,1,0:T(8,128)(2,1)} %param.8) | copy-start | bytes 393220
  138.9 87.6 %copy-start.6 = (u32[128]{0:T(128)S(1)}, u32[128]{0:T(128)}, u32[]{:S(2)}) copy-start(u32[128]{0:T(128)} %constant.18) | copy-start | bytes 1540
  138.9 88.2 %copy-start.5 = (s32[2048]{0:T(1024)S(1)}, s32[2048]{0:T(1024)}, u32[]{:S(2)}) copy-start(s32[2048]{0:T(1024)} %param.13) | copy-start | bytes 24580
  226.5 504.5 %all-reduce.12.cloned.1.call-start = ((), (), s32[]{:S(2)}) async-start(), calls=%async_computation.2 | async-start | bytes 2097152 | tf_op jit(solution)/shard_map/psum | solution.py:31
  371.9 355.7 %copy-start.2 = (f32[256,128]{0,1:T(8,128)S(1)}, f32[256,128]{0,1:T(8,128)}, u32[]{:S(2)}) copy-start(f32[256,128]{0,1:T(8,128)} %all-reduce.8.cloned.1.call-done) | copy-start | bytes 393220
  371.9 355.7 %copy-start.3 = (f32[256,128]{0,1:T(8,128)S(1)}, f32[256,128]{0,1:T(8,128)}, u32[]{:S(2)}) copy-start(f32[256,128]{0,1:T(8,128)} %get-tuple-element.9) | copy-start | bytes 393220
Sparse Core Ops, SparseCore 0:
  11.1 117.7 all-reduce.7
  132.1 92.1 all-reduce.9
  227.5 117.9 all-reduce.13
  348.6 105.5 all-reduce.11
where the time goes:
time: 741 us; the launch traced here: 740 us
  blocking collectives  356 us (48%)
  waiting for transfers between devices  323 us (44%)
  matrix products  27.3 us (4%)
  local copies, waits for them, and re-layouts  15 us (2%)
  between operations  14.7 us (2%)
    unnamed x1, blocking collectives  356 us
    psum x2, waiting for transfers between devices, solve_panel(): return lax.psum(partial_value, 'row')  237 us
    psum x2, waiting for transfers between devices, shards(): lax.psum(panel_term(panels[section], solved_now.astype(jnp.bfloat16)), 'c...  85.3 us
  transfers between devices with their start and end apart: 4, of which 3 were waited for; matrix products, arithmetic and copies ran while one was open for 5% of the time, Pallas kernels for 0%

commit v1 on v0

v1 whole, which is shorter than its diff:
```python
import jax
import jax.numpy as jnp
from jax import lax
from jax.experimental import pallas as pl
from jax.experimental.pallas import tpu as pltpu
from jax.sharding import PartitionSpec as P

MESH = pl.DeviceIdType.MESH
F32 = jnp.float32
BF16 = jnp.bfloat16
SNPS = 16384
CHIPS = 8
COLS = 8
UNIT = 512


def dot(a, b):
    return jnp.dot(a, b, preferred_element_type=F32)


def dot_nt(a, b):
    return lax.dot_general(a, b, (((1,), (1,)), ((), ())), preferred_element_type=F32)


def kernel(
    first_ref, residual, diag, panels, probe, geno, annot,
    trailing, solved, grm,
    res_v, diag_v, pan_v, probe_v, pt_v, geno_v, ann_v,
    half_s, core_r, chip_r, full_s, full_r,
    u_r, t0_v, t_s, t_r, upd_v,
    lo_s, lo_r, l_s, l_r, lf_v, lfo_v, w_v,
    za_s, za_r, zd_s, zc_s, zb_r, xs_s, xs_r, xown_v, c0_v, zx_s, zx_r,
    xa_s, xa_r, xd_s, xc_s, xb_r, out_v, sol_v, trail_v,
    in_sem, geno_sem, out_sem,
    core_sem, chip_sem, full_sem, u_sem, t_sem, upd_sem,
    lo_sem, l_sem, lf_sem, lfo_sem, za_sem, zb_sem, xs_sem, zx_sem, xa_sem, xb_sem,
):
    row, col = lax.axis_index("row"), lax.axis_index("col")
    chip, core = lax.div(row, 2), lax.rem(row, 2)
    zpos, xhi = lax.div(col, 2), lax.rem(col, 2)

    def mate():
        return (chip * 2 + (1 - core), col)

    def chip_at(offset):
        return (lax.rem(chip + offset, CHIPS) * 2 + core, col)

    def col_at(offset):
        return (row, lax.rem(col + offset, COLS))

    def z_at(offset):
        return (row, lax.rem(zpos + offset, 4) * 2 + xhi)

    def x_mate():
        return (row, zpos * 2 + (1 - xhi))

    pending = []

    def remote(src, dst, sems, index, to):
        copy = pltpu.make_async_remote_copy(
            src_ref=src, dst_ref=dst, send_sem=sems.at[0, index], recv_sem=sems.at[1, index],
            device_id=to, device_id_type=MESH,
        )
        return copy

    def send(src, dst, sems, index, to):
        copy = remote(src, dst, sems, index, to)
        copy.start()
        pending.append(copy)
        return copy

    def local(src, dst, sem):
        copy = pltpu.make_async_copy(src, dst, sem)
        copy.start()
        return copy

    c_res = local(residual, res_v, in_sem.at[0])
    c_diag = local(diag, diag_v, in_sem.at[1])
    c_probe = local(probe, probe_v, in_sem.at[2])
    c_geno = []
    for g in range(8):
        base = (1 - core) * 1024 if g < 4 else core * 1024
        start = pl.multiple_of(base + (g % 4) * 256, 256)
        c_geno.append(local(geno.at[:, pl.ds(start, 256)], geno_v.at[:, pl.ds(g * 256, 256)], geno_sem.at[g]))
    c_pan = local(panels, pan_v, in_sem.at[3])
    other8 = pl.multiple_of((1 - core) * 8, 8)
    own8 = pl.multiple_of(core * 8, 8)
    c_ann0 = local(annot.at[pl.ds(other8, 8)], ann_v.at[pl.ds(0, 8)], in_sem.at[4])
    c_ann1 = local(annot.at[pl.ds(own8, 8)], ann_v.at[pl.ds(8, 8)], in_sem.at[5])

    barrier = pltpu.get_barrier_semaphore()
    pl.semaphore_signal(barrier, inc=1, device_id=mate(), device_id_type=MESH)
    for d in range(1, CHIPS):
        pl.semaphore_signal(barrier, inc=1, device_id=chip_at(d), device_id_type=MESH)
    for d in range(1, COLS):
        pl.semaphore_signal(barrier, inc=1, device_id=col_at(d), device_id_type=MESH)

    block = first_ref[0]

    def solve_begin(s, values):
        partial = dot(diag_v[s], values.astype(BF16))
        half_s[s, 0] = partial[:128]
        half_s[s, 1] = partial[128:]

    def solve_core(s):
        send(half_s.at[s, 1 - core], core_r.at[s], core_sem, s, mate())

    def solve_chips(s):
        remote(core_r.at[s], core_r.at[s], core_sem, s, mate()).wait_recv()
        chip_r[s, chip] = (half_s[s, core] + core_r[s]).astype(BF16)
        for d in range(1, CHIPS):
            send(chip_r.at[s, chip], chip_r.at[s, chip], chip_sem, s * 8 + d, chip_at(d))

    def solve_sum(s):
        for d in range(1, CHIPS):
            slot = lax.rem(chip + CHIPS - d, CHIPS)
            remote(chip_r.at[s, slot], chip_r.at[s, slot], chip_sem, s * 8 + d, chip_at(d)).wait_recv()
        total = chip_r[s, 0].astype(F32)
        for p in range(1, CHIPS):
            total = total + chip_r[s, p].astype(F32)
        full_s[s] = total
        send(full_s.at[s], full_r.at[s], full_sem, s, mate())

    def solve_end(s):
        remote(full_s.at[s], full_r.at[s], full_sem, s, mate()).wait_recv()
        sol_v[s, core] = full_s[s]
        sol_v[s, 1 - core] = full_r[s]
        return jnp.concatenate([sol_v[s, 0], sol_v[s, 1]], axis=0).astype(BF16)

    c_res.wait()
    c_diag.wait()
    solve_begin(0, res_v[block])
    c_probe.wait()
    pt_v[...] = probe_v[...].T

    for g in range(4):
        c_geno[g].wait()
        part = dot(pt_v[...], geno_v[:, pl.ds(g * 256, 256)]).astype(BF16)
        lo_s[g, :, :] = part
        if g == 0:
            pl.semaphore_wait(barrier, 15)
            solve_core(0)
        send(lo_s.at[g], lo_r.at[g], lo_sem, g, mate())
        if g == 1:
            solve_chips(0)
    for g in range(4):
        c_geno[4 + g].wait()
        part = dot(pt_v[...], geno_v[:, pl.ds((4 + g) * 256, 256)])
        remote(lo_s.at[g], lo_r.at[g], lo_sem, g, mate()).wait_recv()
        part = (part + lo_r[g].astype(F32)).astype(BF16)
        for h in range(2):
            p = 2 * g + h
            l_s[p] = part[:, h * 128:(h + 1) * 128]

            @pl.when(chip != p)
            def _():
                d = lax.rem(p + CHIPS - chip, CHIPS)
                remote(l_s.at[p], l_r.at[d], l_sem, d, (p * 2 + core, col)).start()

    solve_sum(0)

    total = l_s[chip].astype(F32)
    for d in range(1, CHIPS):
        remote(l_s.at[0], l_r.at[d], l_sem, d, chip_at(d)).wait_recv()
        total = total + l_r[d].astype(F32)
    lf_v[chip] = (total * (1.0 / SNPS)).astype(BF16)
    for d in range(1, CHIPS):
        send(lf_v.at[chip], lf_v.at[chip], lf_sem, d, chip_at(d))
    send(lf_v.at[chip], lfo_v.at[chip], lfo_sem, 0, mate())

    solved0 = solve_end(0)
    c_pan.wait()
    u_r[col] = dot(pan_v[0, block + 1], solved0).astype(BF16)
    for d in range(1, COLS):
        send(u_r.at[col], u_r.at[col], u_sem, d, col_at(d))
    for j in range(COLS):
        for h in range(2):
            b = 2 * j + h
            keep = jnp.where(b > block, 1.0, 0.0).astype(F32)
            t0_v[j, h * 128:(h + 1) * 128] = dot(pan_v[0, b], solved0) * keep

    for d in range(1, CHIPS):
        slot = lax.rem(chip + CHIPS - d, CHIPS)
        remote(lf_v.at[slot], lf_v.at[slot], lf_sem, d, chip_at(d)).wait_recv()
        send(lf_v.at[slot], lfo_v.at[slot], lfo_sem, d, mate())

    z_off = (2, 1, 3, 0)
    c_ann0.wait()
    c_ann1.wait()

    def build(chunk, value):
        ids = ann_v[pl.ds(chunk, 1), :]
        for s in range(4):
            for side in range(2):
                owner = lax.rem(zpos + z_off[s], 4) * 2 + (xhi if side == 0 else 1 - xhi)
                mask = jnp.where(ids == owner, 1.0, 0.0).astype(BF16)
                w_v[s, side * 128:(side + 1) * 128, chunk * 128:(chunk + 1) * 128] = value * mask

    for p in range(CHIPS):
        build(8 + p, lf_v[p])
    for d in range(CHIPS):
        slot = lax.rem(chip + CHIPS - d, CHIPS)
        remote(lf_v.at[slot], lfo_v.at[slot], lfo_sem, d, mate()).wait_recv()
    for p in range(CHIPS):
        build(p, lfo_v[p])

    def unit(b, s):
        return dot_nt(geno_v[pl.ds(b * UNIT, UNIT), :], w_v[s])

    Z2, ZP, ZM, Z0 = 0, 1, 2, 3

    def x_first(b, s):
        value = unit(2 + b, s)
        xown_v[b, s] = value[:, :128]
        xs_s[b, s] = value[:, 128:].astype(BF16)
        send(xs_s.at[b, s], xs_r.at[b, s], xs_sem, b * 4 + s, x_mate())

    def x_arrived(b, s):
        remote(xs_s.at[b, s], xs_r.at[b, s], xs_sem, b * 4 + s, x_mate()).wait_recv()
        return xown_v[b, s] + xs_r[b, s].astype(F32)

    za_s[0] = unit(0, Z2).astype(BF16)
    send(za_s.at[0], za_r.at[0], za_sem, 0, z_at(1))
    za_s[1] = unit(1, Z2).astype(BF16)
    send(za_s.at[1], za_r.at[1], za_sem, 1, z_at(3))
    x_first(0, Z2)

    for d in range(1, COLS):
        slot = lax.rem(col + COLS - d, COLS)
        remote(u_r.at[slot], u_r.at[slot], u_sem, d, col_at(d)).wait_recv()
    u_total = u_r[0].astype(F32)
    for j in range(1, COLS):
        u_total = u_total + u_r[j].astype(F32)
    solve_begin(1, res_v[block + 1] - u_total)
    solve_core(1)

    x_first(1, Z2)
    solve_chips(1)

    zd_s[0] = unit(1, ZP).astype(BF16)
    send(zd_s.at[0], zb_r.at[0, 1], zb_sem, 1, z_at(1))
    zd_s[1] = unit(0, ZM).astype(BF16)
    send(zd_s.at[1], zb_r.at[1, 0], zb_sem, 2, z_at(3))
    x_first(0, ZP)
    x_first(1, ZP)
    solve_sum(1)
    x_first(0, ZM)
    solved1 = solve_end(1)
    for j in range(COLS):
        for h in range(2):
            b = 2 * j + h
            keep = jnp.where(b > block + 1, 1.0, 0.0).astype(F32)
            rows = pl.ds(h * 128, 128)
            t_s[j, rows] = (t0_v[j, rows] + dot(pan_v[1, b], solved1) * keep).astype(BF16)
    for d in range(1, COLS):
        to = lax.rem(col + d, COLS)
        send(t_s.at[to], t_r.at[d], t_sem, d, (row, to))
    x_first(1, ZM)

    value = unit(0, ZP)
    remote(za_s.at[0], za_r.at[0], za_sem, 0, z_at(1)).wait_recv()
    zc_s[0] = (value + za_r[0].astype(F32)).astype(BF16)
    send(zc_s.at[0], zb_r.at[0, 0], zb_sem, 0, z_at(1))
    value = unit(1, ZM)
    remote(za_s.at[1], za_r.at[1], za_sem, 1, z_at(3)).wait_recv()
    zc_s[1] = (value + za_r[1].astype(F32)).astype(BF16)
    send(zc_s.at[1], zb_r.at[1, 1], zb_sem, 3, z_at(3))

    x_first(0, Z0)
    x_first(1, Z0)

    xa_s[0] = x_arrived(0, Z2).astype(BF16)
    send(xa_s.at[0], xa_r.at[0], xa_sem, 0, z_at(1))
    xa_s[1] = x_arrived(1, Z2).astype(BF16)
    send(xa_s.at[1], xa_r.at[1], xa_sem, 1, z_at(3))
    xd_s[0] = x_arrived(1, ZP).astype(BF16)
    send(xd_s.at[0], xb_r.at[0, 1], xb_sem, 1, z_at(1))
    xd_s[1] = x_arrived(0, ZM).astype(BF16)
    send(xd_s.at[1], xb_r.at[1, 0], xb_sem, 2, z_at(3))

    total = t_s[col].astype(F32)
    for d in range(1, COLS):
        remote(t_s.at[0], t_r.at[d], t_sem, d, col_at(d)).wait_recv()
        total = total + t_r[d].astype(F32)
    upd_v[col] = total.astype(BF16)
    for d in range(1, COLS):
        send(upd_v.at[col], upd_v.at[col], upd_sem, d, col_at(d))

    c0_v[0] = unit(0, Z0)
    c0_v[1] = unit(1, Z0)

    def z_arrived(b):
        for way in range(2):
            remote(zc_s.at[0], zb_r.at[way, b], zb_sem, way * 2 + b, z_at(1)).wait_recv()
        sums = c0_v[b] + zb_r[0, b].astype(F32) + zb_r[1, b].astype(F32)
        c0_v[b] = sums
        zx_s[b] = sums[:, 128:].astype(BF16)
        send(zx_s.at[b], zx_r.at[b], zx_sem, b, x_mate())

    z_arrived(1)
    z_arrived(0)

    value = x_arrived(0, ZP)
    remote(xa_s.at[0], xa_r.at[0], xa_sem, 0, z_at(1)).wait_recv()
    xc_s[0] = (value + xa_r[0].astype(F32)).astype(BF16)
    send(xc_s.at[0], xb_r.at[0, 0], xb_sem, 0, z_at(1))
    value = x_arrived(1, ZM)
    remote(xa_s.at[1], xa_r.at[1], xa_sem, 1, z_at(3)).wait_recv()
    xc_s[1] = (value + xa_r[1].astype(F32)).astype(BF16)
    send(xc_s.at[1], xb_r.at[1, 1], xb_sem, 3, z_at(3))

    outs = [local(sol_v, solved, out_sem.at[0])]

    for d in range(1, COLS):
        slot = lax.rem(col + COLS - d, COLS)
        remote(upd_v.at[slot], upd_v.at[slot], upd_sem, d, col_at(d)).wait_recv()
    for j in range(COLS):
        for h in range(2):
            rows = pl.ds(h * 128, 128)
            trail_v[2 * j + h] = res_v[2 * j + h] - upd_v[j, rows].astype(F32)
    outs.append(local(trail_v, trailing, out_sem.at[1]))

    def emit(b, value):
        rows = pl.ds(b * UNIT, UNIT)
        out_v[rows, :] = value.astype(BF16)
        outs.append(local(out_v.at[rows], grm.at[rows], out_sem.at[2 + b]))

    for b in range(2):
        remote(zx_s.at[b], zx_r.at[b], zx_sem, b, x_mate()).wait_recv()
        emit(b, c0_v[b, :, :128] + zx_r[b].astype(F32))
    for b in range(2):
        value = x_arrived(b, Z0)
        for way in range(2):
            remote(xc_s.at[0], xb_r.at[way, b], xb_sem, way * 2 + b, z_at(1)).wait_recv()
            value = value + xb_r[way, b].astype(F32)
        emit(2 + b, value)

    for copy in pending:
        copy.wait_send()
    for d in range(1, CHIPS):
        remote(l_s.at[0], l_r.at[d], l_sem, d, chip_at(d)).wait_send()
    for copy in outs:
        copy.wait()


def shards(residual, diag_inverse, panels, first_block, probe_solved, genotypes, annotation):
    blocks, per_row, rhs = residual.shape
    rows = blocks * per_row
    snps = genotypes.shape[2]
    vmem = pltpu.VMEM
    sem = pltpu.SemaphoreType.DMA
    anywhere = pl.BlockSpec(memory_space=pl.ANY)
    scratch = [
        vmem((16, 128, 128), F32), vmem((2, 256, 128), BF16), vmem((2, 16, 128, 256), BF16),
        vmem((rows, rhs), BF16), vmem((rhs, rows), BF16), vmem((rows, snps), BF16), vmem((16, 128), jnp.int32),
        vmem((2, 2, 128, 128), F32), vmem((2, 128, 128), F32), vmem((2, 8, 128, 128), BF16),
        vmem((2, 128, 128), F32), vmem((2, 128, 128), F32),
        vmem((8, 128, 128), BF16), vmem((8, 256, 128), F32), vmem((8, 256, 128), BF16), vmem((8, 256, 128), BF16),
        vmem((8, 256, 128), BF16),
        vmem((4, 128, 256), BF16), vmem((4, 128, 256), BF16), vmem((8, 128, 128), BF16), vmem((8, 128, 128), BF16),
        vmem((8, 128, 128), BF16), vmem((8, 128, 128), BF16), vmem((4, 256, snps), BF16),
        vmem((2, UNIT, 256), BF16), vmem((2, UNIT, 256), BF16), vmem((2, UNIT, 256), BF16), vmem((2, UNIT, 256), BF16),
        vmem((2, 2, UNIT, 256), BF16), vmem((2, 4, UNIT, 128), BF16), vmem((2, 4, UNIT, 128), BF16),
        vmem((2, 4, UNIT, 128), F32), vmem((2, UNIT, 256), F32), vmem((2, UNIT, 128), BF16), vmem((2, UNIT, 128), BF16),
        vmem((2, UNIT, 128), BF16), vmem((2, UNIT, 128), BF16), vmem((2, UNIT, 128), BF16), vmem((2, UNIT, 128), BF16),
        vmem((2, 2, UNIT, 128), BF16), vmem((rows, rhs), BF16), vmem((2, 2, 128, 128), F32), vmem((16, 128, 128), F32),
        sem((6,)), sem((8,)), sem((6,)),
        sem((2, 2)), sem((2, 16)), sem((2, 2)), sem((2, 8)), sem((2, 8)), sem((2, 8)),
        sem((2, 4)), sem((2, 8)), sem((2, 8)), sem((2, 8)), sem((2, 2)), sem((2, 4)), sem((2, 8)), sem((2, 2)),
        sem((2, 2)), sem((2, 4)),
    ]
    trailing, solved, grm = pl.pallas_call(
        kernel,
        out_shape=(
            jax.ShapeDtypeStruct((blocks, per_row, rhs), F32),
            jax.ShapeDtypeStruct((2, 2, 128, 128), F32),
            jax.ShapeDtypeStruct((rows, rhs), BF16),
        ),
        in_specs=[pl.BlockSpec(memory_space=pltpu.SMEM)] + [anywhere] * 6,
        out_specs=(anywhere,) * 3,
        scratch_shapes=scratch,
        compiler_params=pltpu.CompilerParams(
            collective_id=0, has_side_effects=True, vmem_limit_bytes=56 * 1024 * 1024
        ),
        cost_estimate=pl.CostEstimate(flops=10_000_000_000, bytes_accessed=14_000_000, transcendentals=0),
    )(
        first_block, residual, diag_inverse, panels, probe_solved.reshape(rows, rhs),
        genotypes.reshape(rows, snps), annotation.reshape(16, 128),
    )
    return (
        trailing,
        solved.reshape(2, 256, 128),
        grm.reshape(blocks, per_row, 1, rhs),
    )


def solution(mesh):
    in_specs = (
        P(None, "row", None),
        P(None, "col", "row"),
        P(None, None, "row", "col"),
        P(),
        P(None, "row", None),
        P(None, "row", "col"),
        P("col"),
    )
    out_specs = (P(None, "row", None), P(None, "col", None), P(None, "row", "col", None))
    return jax.shard_map(shards, mesh=mesh, in_specs=in_specs, out_specs=out_specs, check_vma=False)
```

time: 741 us -> 83 us (0.11)
  blocking collectives: 356 us -> 0 us
  waiting for transfers between devices: 323 us -> 0 us
  Pallas kernels: 0 us -> 74.9 us
  matrix products: 27.3 us -> 0 us
  between operations: 14.7 us -> 1.29 us
  local copies, waits for them, and re-layouts: 15 us -> 5.85 us
    unnamed x1 -> x0, blocking collectives: 356 us -> none
    psum x4 -> x0, waiting for transfers between devices: 323 us -> none  [the longest x2 237 us: solve_panel(): return lax.psum(partial_value, 'row')]
    pallas_call x0 -> x1, Pallas kernels: none -> 74.9 us  [shards(): pl.pallas_call(kernel, out_shape=(jax.ShapeDtypeStruct((blocks, per_row,...]
    dot_general x6 -> x0, matrix products: 27.3 us -> none  [the longest x1 12.4 us: shards(): jnp.einsum('ngs,sk->ngk', genotypes, weights, preferred_element_type=jnp....]
    reshape x1 -> x0, local copies, waits for them, and re-layouts: 9.28 us -> none  [shards(): annotated.reshape(genotypes.shape[0], genotypes.shape[1], A, rounded.shap...]
  transfers between devices with their start and end apart: 4 -> 0, of which waited for: 3 -> 0; matrix products, arithmetic and copies ran while one was open for 5% -> 0% of each run, Pallas kernels for 0% -> 0%
where the time goes in v1:
time: 83 us; the launch traced here: 82.1 us
  Pallas kernels  74.9 us (90%)
  local copies, waits for them, and re-layouts  5.85 us (7%)
  between operations  1.29 us (2%)
    pallas_call x1, Pallas kernels, shards(): pl.pallas_call(kernel, out_shape=(jax.ShapeDtypeStruct((blocks, per_row,...  74.9 us
    unnamed x3, local copies, waits for them, and re-layouts  5.85 us

profile of v1, /device:TPU:0, one launch (start us, length us, event | category | flops | bytes accessed | tf_op | source)
XLA Modules:
  0.0 82.1 jit_solution(829150844876851229)
XLA Ops:
  1.3 74.9 %shard_map.94 = (f32[16,128,128]{2,1,0:T(8,128)}, f32[2,2,128,128]{3,2,1,0:T(8,128)}, bf16[2048,128]{1,0:T(8,128)(2,1)}) custom-call(s32[1]{0:T(128)S(6)} %copy.14.first_ref, f32[16,128,128]{2,1,0:T(8,128)} %residual.1, bf16[2,256,128]{2,1,0:T(8,128)(2,1)} %diag.1, bf16[2,16,128,256]{3,2,1,0:T(8,128)(2,1)} %panels.1, bf16[2048,128]{1,0:T(8,128)(2,1)} %bitcast.10, ...), custom_call_target="tpu_custom_call" | custom-call | flops 10000000000 | bytes 14000000 | tf_op jit(solution)/shard_map/pallas_call | solution.py:372
  76.2 2.3 %copy.15 = f32[16,128,128]{2,1,0:T(8,128)} copy(f32[16,128,128]{2,1,0:T(8,128)} %get-tuple-element.15) | data formatting | bytes 2097152
  78.5 1.7 %copy.16 = f32[2,256,128]{2,1,0:T(8,128)} copy(f32[2,256,128]{2,1,0:T(8,128)} %bitcast.8) | data formatting | bytes 524288
  80.2 1.9 %copy.17 = bf16[16,128,1,128]{3,1,2,0:T(8,128)(2,1)} copy(bf16[16,128,1,128]{3,1,2,0:T(8,128)(2,1)} %bitcast.7) | data formatting | bytes 1048576

commit v2 on v1

v2 whole, which is shorter than its diff:
```python
import jax
import jax.numpy as jnp
from jax import lax
from jax.experimental import pallas as pl
from jax.experimental.pallas import tpu as pltpu
from jax.sharding import PartitionSpec as P

MESH = pl.DeviceIdType.MESH
F32 = jnp.float32
BF16 = jnp.bfloat16
SNPS = 16384
CHIPS = 8
COLS = 8
UNIT = 512


def dot(a, b):
    return jnp.dot(a, b, preferred_element_type=F32)


def dot_nt(a, b):
    return lax.dot_general(a, b, (((1,), (1,)), ((), ())), preferred_element_type=F32)


def kernel(
    first_ref, residual, diag, panels, probe, geno, annot,
    trail_v, sol_v, out_v,
    res_v, diag_v, pan_v, probe_v, pt_v, geno_v, ann_v,
    half_s, core_r, chip_r, full_s, full_r,
    u_s, u_x, u_r, t0_v, t_s, t_r, tx_s, tx_r, upd_v,
    lo_s, lo_r, lp_v, l_s, l_r, lf_v, lfo_v, w_v,
    za_s, za_r, zd_s, zc_s, zb_r, xs_s, xs_r, xown_v, c0_v, zx_s, zx_r,
    xa_s, xa_r, xd_s, xc_s, xb_r,
    in_sem, geno_sem,
    core_sem, chip_sem, full_sem, ux_sem, u_sem, t_sem, tx_sem, upd_sem,
    lo_sem, l_sem, lf_sem, lfo_sem, za_sem, zb_sem, xs_sem, zx_sem, xa_sem, xb_sem,
):
    row, col = lax.axis_index("row"), lax.axis_index("col")
    chip, core = lax.div(row, 2), lax.rem(row, 2)
    zpos, xhi = lax.div(col, 2), lax.rem(col, 2)

    def mate():
        return (chip * 2 + (1 - core), col)

    def chip_at(offset):
        return (lax.rem(chip + offset, CHIPS) * 2 + core, col)

    def z_at(offset):
        return (row, lax.rem(zpos + offset, 4) * 2 + xhi)

    def x_mate():
        return (row, zpos * 2 + (1 - xhi))

    pending = []

    def remote(src, dst, sems, index, to):
        return pltpu.make_async_remote_copy(
            src_ref=src, dst_ref=dst, send_sem=sems.at[0, index], recv_sem=sems.at[1, index],
            device_id=to, device_id_type=MESH,
        )

    def send(src, dst, sems, index, to):
        copy = remote(src, dst, sems, index, to)
        copy.start()
        pending.append(copy)

    def local(src, dst, sem):
        copy = pltpu.make_async_copy(src, dst, sem)
        copy.start()
        return copy

    barrier = pltpu.get_barrier_semaphore()
    for d in range(1, CHIPS):
        pl.semaphore_signal(barrier, inc=1, device_id=chip_at(d), device_id_type=MESH)
    for d in range(1, 4):
        pl.semaphore_signal(barrier, inc=1, device_id=z_at(d), device_id_type=MESH)
    pl.semaphore_signal(barrier, inc=1, device_id=x_mate(), device_id_type=MESH)
    pl.semaphore_signal(barrier, inc=1, device_id=mate(), device_id_type=MESH)

    c_probe = local(probe, probe_v, in_sem.at[2])
    c_geno = []
    for g in range(8):
        base = (1 - core) * 1024 if g < 4 else core * 1024
        start = pl.multiple_of(base + (g % 4) * 256, 256)
        c_geno.append(local(geno.at[:, pl.ds(start, 256)], geno_v.at[:, pl.ds(g * 256, 256)], geno_sem.at[g]))
    c_res = local(residual, res_v, in_sem.at[0])
    c_diag = local(diag, diag_v, in_sem.at[1])
    other8 = pl.multiple_of((1 - core) * 8, 8)
    own8 = pl.multiple_of(core * 8, 8)
    c_ann0 = local(annot.at[pl.ds(other8, 8)], ann_v.at[pl.ds(0, 8)], in_sem.at[4])
    c_ann1 = local(annot.at[pl.ds(own8, 8)], ann_v.at[pl.ds(8, 8)], in_sem.at[5])
    c_pan = local(panels, pan_v, in_sem.at[3])

    block = first_ref[0]

    def solve_begin(s, values):
        partial = dot(diag_v[s], values.astype(BF16))
        half_s[s, 0] = partial[:128]
        half_s[s, 1] = partial[128:]

    def solve_core(s):
        send(half_s.at[s, 1 - core], core_r.at[s], core_sem, s, mate())

    def solve_chips(s):
        remote(core_r.at[s], core_r.at[s], core_sem, s, mate()).wait_recv()
        chip_r[s, chip] = (half_s[s, core] + core_r[s]).astype(BF16)
        for d in range(1, CHIPS):
            send(chip_r.at[s, chip], chip_r.at[s, chip], chip_sem, s * 8 + d, chip_at(d))

    def solve_sum(s):
        for d in range(1, CHIPS):
            slot = lax.rem(chip + CHIPS - d, CHIPS)
            remote(chip_r.at[s, slot], chip_r.at[s, slot], chip_sem, s * 8 + d, chip_at(d)).wait_recv()
        total = chip_r[s, 0].astype(F32)
        for p in range(1, CHIPS):
            total = total + chip_r[s, p].astype(F32)
        full_s[s] = total
        send(full_s.at[s], full_r.at[s], full_sem, s, mate())

    def solve_end(s):
        remote(full_s.at[s], full_r.at[s], full_sem, s, mate()).wait_recv()
        sol_v[s, core] = full_s[s]
        sol_v[s, 1 - core] = full_r[s]
        return jnp.concatenate([sol_v[s, 0], sol_v[s, 1]], axis=0).astype(BF16)

    c_probe.wait()
    pt_v[...] = probe_v[...].T
    for g in range(4):
        c_geno[g].wait()
        lo_s[g] = dot(pt_v[...], geno_v[:, pl.ds(g * 256, 256)]).astype(BF16)
    for g in range(4):
        c_geno[4 + g].wait()
        lp_v[g] = dot(pt_v[...], geno_v[:, pl.ds((4 + g) * 256, 256)])
    c_res.wait()
    c_diag.wait()
    solve_begin(0, res_v[block])
    pl.semaphore_wait(barrier, 12)
    for g in range(4):
        send(lo_s.at[g], lo_r.at[g], lo_sem, g, mate())
    solve_core(0)
    for g in range(4):
        remote(lo_s.at[g], lo_r.at[g], lo_sem, g, mate()).wait_recv()
        part = (lp_v[g] + lo_r[g].astype(F32)).astype(BF16)
        for h in range(2):
            l_s[2 * g + h] = part[:, h * 128:(h + 1) * 128]
    for d in range(1, CHIPS):
        send(l_s.at[lax.rem(chip + d, CHIPS)], l_r.at[d], l_sem, d, chip_at(d))
    solve_chips(0)

    total = l_s[chip].astype(F32)
    for d in range(1, CHIPS):
        remote(l_s.at[0], l_r.at[d], l_sem, d, chip_at(d)).wait_recv()
        total = total + l_r[d].astype(F32)
    lf_v[chip] = (total * (1.0 / SNPS)).astype(BF16)
    for d in range(1, CHIPS):
        send(lf_v.at[chip], lf_v.at[chip], lf_sem, d, chip_at(d))
    send(lf_v.at[chip], lfo_v.at[chip], lfo_sem, 0, mate())

    solve_sum(0)
    c_ann0.wait()
    c_ann1.wait()
    c_pan.wait()
    solved0 = solve_end(0)
    u_s[...] = dot(pan_v[0, block + 1], solved0).astype(BF16)
    send(u_s, u_x, ux_sem, 0, x_mate())

    z_off = (2, 1, 3, 0)

    def build(half, chunk, value):
        ids = ann_v[pl.ds(half * 8 + chunk, 1), :]
        lanes = pl.ds(pl.multiple_of(half * 1024 + chunk * 128, 128), 128)
        for s in range(4):
            for side in range(2):
                owner = lax.rem(zpos + z_off[s], 4) * 2 + (xhi if side == 0 else 1 - xhi)
                mask = jnp.where(ids == owner, 1.0, 0.0).astype(BF16)
                w_v[s, side * 128:(side + 1) * 128, lanes] = value * mask

    build(1, chip, lf_v[chip])
    for d in range(1, CHIPS):
        slot = lax.rem(chip + CHIPS - d, CHIPS)
        remote(lf_v.at[slot], lf_v.at[slot], lf_sem, d, chip_at(d)).wait_recv()
        send(lf_v.at[slot], lfo_v.at[slot], lfo_sem, d, mate())
        build(1, slot, lf_v[slot])
    remote(u_s, u_x, ux_sem, 0, x_mate()).wait_recv()
    u_r[zpos] = (u_s[...].astype(F32) + u_x[...].astype(F32)).astype(BF16)
    for d in range(1, 4):
        send(u_r.at[zpos], u_r.at[zpos], u_sem, d, z_at(d))
    for d in range(CHIPS):
        slot = lax.rem(chip + CHIPS - d, CHIPS)
        remote(lf_v.at[slot], lfo_v.at[slot], lfo_sem, d, mate()).wait_recv()
        build(0, slot, lfo_v[slot])

    def unit(b, s):
        return dot_nt(geno_v[pl.ds(b * UNIT, UNIT), :], w_v[s])

    Z2, ZP, ZM, Z0 = 0, 1, 2, 3

    def x_first(b, s):
        value = unit(2 + b, s)
        xown_v[b, s] = value[:, :128]
        xs_s[b, s] = value[:, 128:].astype(BF16)
        send(xs_s.at[b, s], xs_r.at[b, s], xs_sem, b * 4 + s, x_mate())

    def x_arrived(b, s):
        remote(xs_s.at[b, s], xs_r.at[b, s], xs_sem, b * 4 + s, x_mate()).wait_recv()
        return xown_v[b, s] + xs_r[b, s].astype(F32)

    za_s[0] = unit(0, Z2).astype(BF16)
    send(za_s.at[0], za_r.at[0], za_sem, 0, z_at(1))
    x_first(0, Z2)
    za_s[1] = unit(1, Z2).astype(BF16)
    send(za_s.at[1], za_r.at[1], za_sem, 1, z_at(3))
    x_first(1, Z2)

    for d in range(1, 4):
        slot = lax.rem(zpos + 4 - d, 4)
        remote(u_r.at[slot], u_r.at[slot], u_sem, d, z_at(d)).wait_recv()
    u_total = u_r[0].astype(F32)
    for j in range(1, 4):
        u_total = u_total + u_r[j].astype(F32)
    solve_begin(1, res_v[block + 1] - u_total)
    solve_core(1)

    zd_s[0] = unit(1, ZP).astype(BF16)
    send(zd_s.at[0], zb_r.at[0, 1], zb_sem, 1, z_at(1))
    solve_chips(1)
    x_first(1, ZP)
    zd_s[1] = unit(0, ZM).astype(BF16)
    send(zd_s.at[1], zb_r.at[1, 0], zb_sem, 2, z_at(3))
    for j in range(16):
        keep = jnp.where(j > block, 1.0, 0.0).astype(F32)
        t0_v[j] = dot(pan_v[0, j], solved0) * keep
    x_first(0, ZM)

    value = unit(0, ZP)
    remote(za_s.at[0], za_r.at[0], za_sem, 0, z_at(1)).wait_recv()
    zc_s[0] = (value + za_r[0].astype(F32)).astype(BF16)
    send(zc_s.at[0], zb_r.at[0, 0], zb_sem, 0, z_at(1))
    solve_sum(1)
    x_first(0, ZP)
    value = unit(1, ZM)
    remote(za_s.at[1], za_r.at[1], za_sem, 1, z_at(3)).wait_recv()
    zc_s[1] = (value + za_r[1].astype(F32)).astype(BF16)
    send(zc_s.at[1], zb_r.at[1, 1], zb_sem, 3, z_at(3))

    solved1 = solve_end(1)
    for j in range(16):
        keep = jnp.where(j > block + 1, 1.0, 0.0).astype(F32)
        t_s[j // 4, j % 4] = (t0_v[j] + dot(pan_v[1, j], solved1) * keep).astype(BF16)
    for d in range(1, 4):
        send(t_s.at[lax.rem(zpos + d, 4)], t_r.at[d], t_sem, d, z_at(d))
    x_first(1, ZM)

    xa_s[0] = x_arrived(0, Z2).astype(BF16)
    send(xa_s.at[0], xa_r.at[0], xa_sem, 0, z_at(1))
    xa_s[1] = x_arrived(1, Z2).astype(BF16)
    send(xa_s.at[1], xa_r.at[1], xa_sem, 1, z_at(3))
    x_first(0, Z0)
    x_first(1, Z0)
    c0_v[0] = unit(0, Z0)
    c0_v[1] = unit(1, Z0)

    total = t_s[zpos].astype(F32)
    for d in range(1, 4):
        remote(t_s.at[0], t_r.at[d], t_sem, d, z_at(d)).wait_recv()
        total = total + t_r[d].astype(F32)
    tx_s[...] = total.astype(BF16)
    send(tx_s, tx_r, tx_sem, 0, x_mate())

    xd_s[0] = x_arrived(1, ZP).astype(BF16)
    send(xd_s.at[0], xb_r.at[0, 1], xb_sem, 1, z_at(1))
    xd_s[1] = x_arrived(0, ZM).astype(BF16)
    send(xd_s.at[1], xb_r.at[1, 0], xb_sem, 2, z_at(3))

    def z_arrived(b):
        for way in range(2):
            remote(zc_s.at[0], zb_r.at[way, b], zb_sem, way * 2 + b, z_at(1)).wait_recv()
        sums = c0_v[b] + zb_r[0, b].astype(F32) + zb_r[1, b].astype(F32)
        c0_v[b] = sums
        zx_s[b] = sums[:, 128:].astype(BF16)
        send(zx_s.at[b], zx_r.at[b], zx_sem, b, x_mate())

    z_arrived(0)
    z_arrived(1)

    remote(tx_s, tx_r, tx_sem, 0, x_mate()).wait_recv()
    upd_v[zpos] = (tx_s[...].astype(F32) + tx_r[...].astype(F32)).astype(BF16)
    for d in range(1, 4):
        send(upd_v.at[zpos], upd_v.at[zpos], upd_sem, d, z_at(d))

    value = x_arrived(0, ZP)
    remote(xa_s.at[0], xa_r.at[0], xa_sem, 0, z_at(1)).wait_recv()
    xc_s[0] = (value + xa_r[0].astype(F32)).astype(BF16)
    send(xc_s.at[0], xb_r.at[0, 0], xb_sem, 0, z_at(1))
    value = x_arrived(1, ZM)
    remote(xa_s.at[1], xa_r.at[1], xa_sem, 1, z_at(3)).wait_recv()
    xc_s[1] = (value + xa_r[1].astype(F32)).astype(BF16)
    send(xc_s.at[1], xb_r.at[1, 1], xb_sem, 3, z_at(3))

    for d in range(1, 4):
        slot = lax.rem(zpos + 4 - d, 4)
        remote(upd_v.at[slot], upd_v.at[slot], upd_sem, d, z_at(d)).wait_recv()
    for j in range(16):
        trail_v[j] = res_v[j] - upd_v[j // 4, j % 4].astype(F32)

    def emit(b, value):
        out_v[pl.ds(b * UNIT, UNIT), :] = value.astype(BF16)

    for b in range(2):
        remote(zx_s.at[b], zx_r.at[b], zx_sem, b, x_mate()).wait_recv()
        emit(b, c0_v[b, :, :128] + zx_r[b].astype(F32))
    for b in range(2):
        value = x_arrived(b, Z0)
        for way in range(2):
            remote(xc_s.at[0], xb_r.at[way, b], xb_sem, way * 2 + b, z_at(1)).wait_recv()
            value = value + xb_r[way, b].astype(F32)
        emit(2 + b, value)

    for copy in pending:
        copy.wait_send()


def store(trail_v, sol_v, out_v, trailing, solved, grm, sems):
    copies = [
        pltpu.make_async_copy(trail_v, trailing, sems.at[0]),
        pltpu.make_async_copy(sol_v, solved, sems.at[1]),
        pltpu.make_async_copy(out_v, grm, sems.at[2]),
    ]
    for copy in copies:
        copy.start()
    for copy in copies:
        copy.wait()


def shards(residual, diag_inverse, panels, first_block, probe_solved, genotypes, annotation):
    blocks, per_row, rhs = residual.shape
    rows = blocks * per_row
    snps = genotypes.shape[2]
    vmem = pltpu.VMEM
    sem = pltpu.SemaphoreType.DMA
    anywhere = pl.BlockSpec(memory_space=pl.ANY)
    in_vmem = pl.BlockSpec(memory_space=pltpu.VMEM)
    scratch = [
        vmem((16, 128, 128), F32), vmem((2, 256, 128), BF16), vmem((2, 16, 128, 256), BF16),
        vmem((rows, rhs), BF16), vmem((rhs, rows), BF16), vmem((rows, snps), BF16), vmem((16, 128), jnp.int32),
        vmem((2, 2, 128, 128), F32), vmem((2, 128, 128), F32), vmem((2, 8, 128, 128), BF16),
        vmem((2, 128, 128), F32), vmem((2, 128, 128), F32),
        vmem((128, 128), BF16), vmem((128, 128), BF16), vmem((4, 128, 128), BF16),
        vmem((16, 128, 128), F32), vmem((4, 4, 128, 128), BF16), vmem((4, 4, 128, 128), BF16),
        vmem((4, 128, 128), BF16), vmem((4, 128, 128), BF16), vmem((4, 4, 128, 128), BF16),
        vmem((4, 128, 256), BF16), vmem((4, 128, 256), BF16), vmem((4, 128, 256), F32),
        vmem((8, 128, 128), BF16), vmem((8, 128, 128), BF16),
        vmem((8, 128, 128), BF16), vmem((8, 128, 128), BF16), vmem((4, 256, snps), BF16),
        vmem((2, UNIT, 256), BF16), vmem((2, UNIT, 256), BF16), vmem((2, UNIT, 256), BF16), vmem((2, UNIT, 256), BF16),
        vmem((2, 2, UNIT, 256), BF16), vmem((2, 4, UNIT, 128), BF16), vmem((2, 4, UNIT, 128), BF16),
        vmem((2, 4, UNIT, 128), F32), vmem((2, UNIT, 256), F32), vmem((2, UNIT, 128), BF16), vmem((2, UNIT, 128), BF16),
        vmem((2, UNIT, 128), BF16), vmem((2, UNIT, 128), BF16), vmem((2, UNIT, 128), BF16), vmem((2, UNIT, 128), BF16),
        vmem((2, 2, UNIT, 128), BF16),
        sem((6,)), sem((8,)),
        sem((2, 2)), sem((2, 16)), sem((2, 2)), sem((2, 1)), sem((2, 4)), sem((2, 4)), sem((2, 1)), sem((2, 4)),
        sem((2, 4)), sem((2, 8)), sem((2, 8)), sem((2, 8)), sem((2, 2)), sem((2, 4)), sem((2, 8)), sem((2, 2)),
        sem((2, 2)), sem((2, 4)),
    ]
    results = (
        jax.ShapeDtypeStruct((blocks, per_row, rhs), F32),
        jax.ShapeDtypeStruct((2, 2, 128, 128), F32),
        jax.ShapeDtypeStruct((rows, rhs), BF16),
    )
    parts = pl.pallas_call(
        kernel,
        out_shape=tuple(pltpu.VMEM(r.shape, r.dtype) for r in results),
        in_specs=[pl.BlockSpec(memory_space=pltpu.SMEM)] + [pl.BlockSpec(memory_space=pltpu.HBM)] * 6,
        out_specs=(in_vmem,) * 3,
        scratch_shapes=scratch,
        compiler_params=pltpu.CompilerParams(
            collective_id=0, has_side_effects=True, vmem_limit_bytes=58 * 1024 * 1024
        ),
        cost_estimate=pl.CostEstimate(flops=10_000_000_000, bytes_accessed=14_000_000, transcendentals=0),
    )(
        first_block, residual, diag_inverse, panels, probe_solved.reshape(rows, rhs),
        genotypes.reshape(rows, snps), annotation.reshape(16, 128),
    )
    trailing, solved, grm = pl.pallas_call(
        store,
        out_shape=results,
        in_specs=[anywhere] * 3,
        out_specs=(anywhere,) * 3,
        scratch_shapes=[sem((3,))],
        compiler_params=pltpu.CompilerParams(vmem_limit_bytes=4 * 1024 * 1024),
    )(*parts)
    return (
        trailing,
        solved.reshape(2, 256, 128),
        grm.reshape(blocks, per_row, 1, rhs),
    )


def solution(mesh):
    in_specs = (
        P(None, "row", None),
        P(None, "col", "row"),
        P(None, None, "row", "col"),
        P(),
        P(None, "row", None),
        P(None, "row", "col"),
        P("col"),
    )
    out_specs = (P(None, "row", None), P(None, "col", None), P(None, "row", "col", None))
    return jax.shard_map(shards, mesh=mesh, in_specs=in_specs, out_specs=out_specs, check_vma=False)
```

time: 83 us -> 71.9 us (0.87); the launches traced: 82.1 us -> 71.8 us
  local copies, waits for them, and re-layouts: 5.85 us -> 0 us
  Pallas kernels: 74.9 us -> 70.4 us
    unnamed x3 -> x0, local copies, waits for them, and re-layouts: 5.85 us -> none
    pallas_call x1 -> x2, Pallas kernels: 74.9 us -> 70.4 us  [the longest x1 69.1 us: shards(): pl.pallas_call(kernel, out_shape=tuple((pltpu.VMEM(r.shape, r.dtype) for...]
where the time goes in v2:
time: 71.9 us; the launch traced here: 71.8 us
  Pallas kernels  70.4 us (98%)
  between operations  1.45 us (2%)
    pallas_call x1, Pallas kernels, shards(): pl.pallas_call(kernel, out_shape=tuple((pltpu.VMEM(r.shape, r.dtype) for...  69.1 us

profile of v2, /device:TPU:0, one launch (start us, length us, event | category | flops | bytes accessed | tf_op | source)
XLA Modules:
  0.0 71.8 jit_solution(14217175812429690251)
XLA Ops:
  1.3 69.1 %shard_map.94 = (f32[16,128,128]{2,1,0:T(8,128)S(1)}, f32[2,2,128,128]{3,2,1,0:T(8,128)S(1)}, bf16[2048,128]{1,0:T(8,128)(2,1)S(1)}) custom-call(s32[1]{0:T(128)S(6)} %copy.11.first_ref, f32[16,128,128]{2,1,0:T(8,128)} %residual.1, bf16[2,256,128]{2,1,0:T(8,128)(2,1)} %diag.1, bf16[2,16,128,256]{3,2,1,0:T(8,128)(2,1)} %panels.1, bf16[2048,128]{1,0:T(8,128)(2,1)} %bitcast.8, ...), custom_call_target="tpu_custom_call" | custom-call | flops 10000000000 | bytes 14000000 | tf_op jit(solution)/shard_map/pallas_call | solution.py:369
  70.4 1.3 %shard_map.95 = (f32[16,128,128]{2,1,0:T(8,128)}, f32[2,2,128,128]{3,2,1,0:T(8,128)}, bf16[2048,128]{1,0:T(8,128)(2,1)}) custom-call(f32[16,128,128]{2,1,0:T(8,128)S(1)} %get-tuple-element.9.trail_v, f32[2,2,128,128]{3,2,1,0:T(8,128)S(1)} %get-tuple-element.10.sol_v, bf16[2048,128]{1,0:T(8,128)(2,1)S(1)} %get-tuple-element.11.out_v), custom_call_target="tpu_custom_call" | custom-call | tf_op jit(solution)/shard_map/pallas_call | solution.py:383

commit v3 on v2

v3 whole, which is shorter than its diff:
```python
import jax
import jax.numpy as jnp
from jax import lax
from jax.experimental import pallas as pl
from jax.experimental.pallas import tpu as pltpu
from jax.sharding import PartitionSpec as P

MESH = pl.DeviceIdType.MESH
F32 = jnp.float32
BF16 = jnp.bfloat16
SNPS = 16384
CHIPS = 8
COLS = 8
ZROWS = 448
XROWS = 576


def dot(a, b):
    return jnp.dot(a, b, preferred_element_type=F32)


def dot_nt(a, b):
    return lax.dot_general(a, b, (((1,), (1,)), ((), ())), preferred_element_type=F32)


def kernel(
    first_ref, residual, diag, panels, probe, geno, annot,
    trail_v, sol_v, out_v,
    res_v, diag_v, pan_v, probe_v, pt_v, geno_v, ann_v,
    half_s, core_r, pair_s, pair_r, chip_r, full_s, full_r,
    u_s, u_x, u_r, t0_v, t_s, t_r, tx_s, tx_r, upd_v,
    lo_s, lo_r, lp_v, l_s, l_r, lf_v, lfo_v, w_v,
    za_s, za_r, zd_s, zc_s, zb_r, xs_s, xs_r, xown_v, c0_v, zx_s, zx_r,
    xa_s, xa_r, xd_s, xc_s, xb_r,
    first_v, in_sem, geno_sem,
    core_sem, pair_sem, chip_sem, full_sem, ux_sem, u_sem, t_sem, tx_sem, upd_sem,
    lo_sem, l_sem, lf_sem, lfo_sem, za_sem, zb_sem, xs_sem, zx_sem, xa_sem, xb_sem,
):
    row, col = lax.axis_index("row"), lax.axis_index("col")
    chip, core = lax.div(row, 2), lax.rem(row, 2)
    zpos, xhi = lax.div(col, 2), lax.rem(col, 2)
    ypos = lax.rem(chip, 4)

    def mate():
        return (chip * 2 + (1 - core), col)

    def chip_at(offset):
        return (lax.rem(chip + offset, CHIPS) * 2 + core, col)

    def y_at(offset):
        return ((lax.div(chip, 4) * 4 + lax.rem(ypos + offset, 4)) * 2 + core, col)

    def z_at(offset):
        return (row, lax.rem(zpos + offset, 4) * 2 + xhi)

    def x_mate():
        return (row, zpos * 2 + (1 - xhi))

    pending = []

    def remote(src, dst, sems, index, to):
        return pltpu.make_async_remote_copy(
            src_ref=src, dst_ref=dst, send_sem=sems.at[0, index], recv_sem=sems.at[1, index],
            device_id=to, device_id_type=MESH,
        )

    def send(src, dst, sems, index, to):
        copy = remote(src, dst, sems, index, to)
        copy.start()
        pending.append(copy)

    def local(src, dst, sem):
        copy = pltpu.make_async_copy(src, dst, sem)
        copy.start()
        return copy

    barrier = pltpu.get_barrier_semaphore()
    for d in range(1, CHIPS):
        pl.semaphore_signal(barrier, inc=1, device_id=chip_at(d), device_id_type=MESH)
    for d in range(1, 4):
        pl.semaphore_signal(barrier, inc=1, device_id=z_at(d), device_id_type=MESH)
    pl.semaphore_signal(barrier, inc=1, device_id=x_mate(), device_id_type=MESH)
    pl.semaphore_signal(barrier, inc=1, device_id=mate(), device_id_type=MESH)

    c_first = local(first_ref, first_v, in_sem.at[6])
    c_probe = local(probe, probe_v, in_sem.at[2])
    c_geno = []
    for g in range(8):
        base = (1 - core) * 1024 if g < 4 else core * 1024
        start = pl.multiple_of(base + (g % 4) * 256, 256)
        c_geno.append(local(geno.at[:, pl.ds(start, 256)], geno_v.at[:, pl.ds(g * 256, 256)], geno_sem.at[g]))
    c_res = local(residual, res_v, in_sem.at[0])
    c_diag = local(diag, diag_v, in_sem.at[1])
    other8 = pl.multiple_of((1 - core) * 8, 8)
    own8 = pl.multiple_of(core * 8, 8)
    c_ann0 = local(annot.at[pl.ds(other8, 8)], ann_v.at[pl.ds(0, 8)], in_sem.at[4])
    c_ann1 = local(annot.at[pl.ds(own8, 8)], ann_v.at[pl.ds(8, 8)], in_sem.at[5])
    c_pan = local(panels, pan_v, in_sem.at[3])

    c_first.wait()
    block = first_v[0]

    def solve_begin(s, values):
        partial = dot(diag_v[s], values.astype(BF16))
        half_s[s, 0] = partial[:128]
        half_s[s, 1] = partial[128:]

    def solve_core(s):
        send(half_s.at[s, 1 - core], core_r.at[s], core_sem, s, mate())

    def solve_pair(s):
        remote(core_r.at[s], core_r.at[s], core_sem, s, mate()).wait_recv()
        pair_s[s] = (half_s[s, core] + core_r[s]).astype(BF16)
        send(pair_s.at[s], pair_r.at[s], pair_sem, s, chip_at(4))

    def solve_y(s):
        remote(pair_s.at[s], pair_r.at[s], pair_sem, s, chip_at(4)).wait_recv()
        chip_r[s, ypos] = (pair_s[s].astype(F32) + pair_r[s].astype(F32)).astype(BF16)
        for d in range(1, 4):
            send(chip_r.at[s, ypos], chip_r.at[s, ypos], chip_sem, s * 4 + d, y_at(d))

    def solve_sum(s):
        for d in range(1, 4):
            slot = lax.rem(ypos + 4 - d, 4)
            remote(chip_r.at[s, slot], chip_r.at[s, slot], chip_sem, s * 4 + d, y_at(d)).wait_recv()
        total = chip_r[s, 0].astype(F32)
        for p in range(1, 4):
            total = total + chip_r[s, p].astype(F32)
        full_s[s] = total
        send(full_s.at[s], full_r.at[s], full_sem, s, mate())

    def solve_end(s):
        remote(full_s.at[s], full_r.at[s], full_sem, s, mate()).wait_recv()
        sol_v[s, core] = full_s[s]
        sol_v[s, 1 - core] = full_r[s]
        return jnp.concatenate([sol_v[s, 0], sol_v[s, 1]], axis=0).astype(BF16)

    c_probe.wait()
    pt_v[...] = probe_v[...].T
    for g in range(4):
        c_geno[g].wait()
        lo_s[g] = dot(pt_v[...], geno_v[:, pl.ds(g * 256, 256)]).astype(BF16)
    c_res.wait()
    c_diag.wait()
    solve_begin(0, res_v[block])
    pl.semaphore_wait(barrier, 12)
    solve_core(0)
    for g in range(4):
        send(lo_s.at[g], lo_r.at[g], lo_sem, g, mate())
    c_geno[4].wait()
    lp_v[0] = dot(pt_v[...], geno_v[:, pl.ds(1024, 256)])
    solve_pair(0)
    c_geno[5].wait()
    lp_v[1] = dot(pt_v[...], geno_v[:, pl.ds(1280, 256)])
    c_geno[6].wait()
    lp_v[2] = dot(pt_v[...], geno_v[:, pl.ds(1536, 256)])
    c_geno[7].wait()
    lp_v[3] = dot(pt_v[...], geno_v[:, pl.ds(1792, 256)])
    for g in range(4):
        remote(lo_s.at[g], lo_r.at[g], lo_sem, g, mate()).wait_recv()
        part = (lp_v[g] + lo_r[g].astype(F32)).astype(BF16)
        for h in range(2):
            p = 2 * g + h
            l_s[p] = part[:, h * 128:(h + 1) * 128]

            @pl.when(chip != p)
            def _():
                d = lax.rem(p + CHIPS - chip, CHIPS)
                remote(l_s.at[p], l_r.at[d], l_sem, d, (p * 2 + core, col)).start()

    solve_y(0)
    total = l_s[chip].astype(F32)
    for d in range(1, CHIPS):
        remote(l_s.at[0], l_r.at[d], l_sem, d, chip_at(d)).wait_recv()
        total = total + l_r[d].astype(F32)
    lf_v[chip] = (total * (1.0 / SNPS)).astype(BF16)
    for d in range(1, CHIPS):
        send(lf_v.at[chip], lf_v.at[chip], lf_sem, d, chip_at(d))
    send(lf_v.at[chip], lfo_v.at[chip], lfo_sem, 0, mate())

    solve_sum(0)
    c_ann0.wait()
    c_ann1.wait()
    c_pan.wait()
    solved0 = solve_end(0)
    u_s[...] = dot(pan_v[0, block + 1], solved0).astype(BF16)
    send(u_s, u_x, ux_sem, 0, x_mate())

    z_off = (2, 1, 3, 0)

    def build(half, chunk, value):
        ids = ann_v[pl.ds(half * 8 + chunk, 1), :]
        lanes = pl.ds(pl.multiple_of(half * 1024 + chunk * 128, 128), 128)
        for s in range(4):
            for side in range(2):
                owner = lax.rem(zpos + z_off[s], 4) * 2 + (xhi if side == 0 else 1 - xhi)
                mask = jnp.where(ids == owner, 1.0, 0.0).astype(BF16)
                w_v[s, side * 128:(side + 1) * 128, lanes] = value * mask

    build(1, chip, lf_v[chip])
    for d in range(1, CHIPS):
        slot = lax.rem(chip + CHIPS - d, CHIPS)
        remote(lf_v.at[slot], lf_v.at[slot], lf_sem, d, chip_at(d)).wait_recv()
        send(lf_v.at[slot], lfo_v.at[slot], lfo_sem, d, mate())
        build(1, slot, lf_v[slot])
    remote(u_s, u_x, ux_sem, 0, x_mate()).wait_recv()
    u_r[zpos] = (u_s[...].astype(F32) + u_x[...].astype(F32)).astype(BF16)
    for d in range(1, 4):
        send(u_r.at[zpos], u_r.at[zpos], u_sem, d, z_at(d))
    for d in range(CHIPS):
        slot = lax.rem(chip + CHIPS - d, CHIPS)
        remote(lf_v.at[slot], lfo_v.at[slot], lfo_sem, d, mate()).wait_recv()
        build(0, slot, lfo_v[slot])

    Z2, ZP, ZM, Z0 = 0, 1, 2, 3

    def z_unit(b, s):
        return dot_nt(geno_v[pl.ds(b * ZROWS, ZROWS), :], w_v[s])

    def xs(b, s):
        value = dot_nt(geno_v[pl.ds(2 * ZROWS + b * XROWS, XROWS), :], w_v[s])
        xown_v[b, s] = value[:, :128]
        xs_s[b, s] = value[:, 128:].astype(BF16)
        send(xs_s.at[b, s], xs_r.at[b, s], xs_sem, b * 4 + s, x_mate())

    def x_arrived(b, s):
        remote(xs_s.at[b, s], xs_r.at[b, s], xs_sem, b * 4 + s, x_mate()).wait_recv()
        return xown_v[b, s] + xs_r[b, s].astype(F32)

    WAY = (1, 3)
    NEAR = (ZP, ZM)

    def za(b):
        za_s[b] = z_unit(b, Z2).astype(BF16)
        send(za_s.at[b], za_r.at[b], za_sem, b, z_at(WAY[b]))

    def zd(b):
        zd_s[b] = z_unit(1 - b, NEAR[b]).astype(BF16)
        send(zd_s.at[b], zb_r.at[b, 1 - b], zb_sem, b * 2 + 1 - b, z_at(WAY[b]))

    def zc(b):
        value = z_unit(b, NEAR[b])
        remote(za_s.at[b], za_r.at[b], za_sem, b, z_at(WAY[b])).wait_recv()
        zc_s[b] = (value + za_r[b].astype(F32)).astype(BF16)
        send(zc_s.at[b], zb_r.at[b, b], zb_sem, b * 2 + b, z_at(WAY[b]))

    def z(b):
        c0_v[b] = z_unit(b, Z0)

    def zx(b):
        for way in range(2):
            remote(zc_s.at[0], zb_r.at[way, b], zb_sem, way * 2 + b, z_at(WAY[way])).wait_recv()
        sums = c0_v[b] + zb_r[0, b].astype(F32) + zb_r[1, b].astype(F32)
        c0_v[b] = sums
        zx_s[b] = sums[:, 128:].astype(BF16)
        send(zx_s.at[b], zx_r.at[b], zx_sem, b, x_mate())

    def xa(b):
        xa_s[b] = x_arrived(b, Z2).astype(BF16)
        send(xa_s.at[b], xa_r.at[b], xa_sem, b, z_at(WAY[b]))

    def xd(b):
        xd_s[b] = x_arrived(1 - b, NEAR[b]).astype(BF16)
        send(xd_s.at[b], xb_r.at[b, 1 - b], xb_sem, b * 2 + 1 - b, z_at(WAY[b]))

    def xc(b):
        value = x_arrived(b, NEAR[b])
        remote(xa_s.at[b], xa_r.at[b], xa_sem, b, z_at(WAY[b])).wait_recv()
        xc_s[b] = (value + xa_r[b].astype(F32)).astype(BF16)
        send(xc_s.at[b], xb_r.at[b, b], xb_sem, b * 2 + b, z_at(WAY[b]))

    def fz(b):
        remote(zx_s.at[b], zx_r.at[b], zx_sem, b, x_mate()).wait_recv()
        out_v[pl.ds(b * ZROWS, ZROWS), :] = (c0_v[b, :, :128] + zx_r[b].astype(F32)).astype(BF16)

    def fx(b):
        value = x_arrived(b, Z0)
        for way in range(2):
            remote(xc_s.at[0], xb_r.at[way, b], xb_sem, way * 2 + b, z_at(WAY[way])).wait_recv()
            value = value + xb_r[way, b].astype(F32)
        out_v[pl.ds(2 * ZROWS + b * XROWS, XROWS), :] = value.astype(BF16)

    def step_begin():
        for d in range(1, 4):
            slot = lax.rem(zpos + 4 - d, 4)
            remote(u_r.at[slot], u_r.at[slot], u_sem, d, z_at(d)).wait_recv()
        total = u_r[0].astype(F32)
        for j in range(1, 4):
            total = total + u_r[j].astype(F32)
        solve_begin(1, res_v[block + 1] - total)
        solve_core(1)

    def update_first():
        for j in range(16):
            keep = jnp.where(j > block, 1.0, 0.0).astype(F32)
            t0_v[j] = dot(pan_v[0, j], solved0) * keep

    def update_scatter():
        solved1 = solve_end(1)
        for j in range(16):
            keep = jnp.where(j > block + 1, 1.0, 0.0).astype(F32)
            t_s[j // 4, j % 4] = (t0_v[j] + dot(pan_v[1, j], solved1) * keep).astype(BF16)
        for d in range(1, 4):
            send(t_s.at[lax.rem(zpos + d, 4)], t_r.at[d], t_sem, d, z_at(d))

    def update_swap():
        total = t_s[zpos].astype(F32)
        for d in range(1, 4):
            remote(t_s.at[0], t_r.at[d], t_sem, d, z_at(d)).wait_recv()
            total = total + t_r[d].astype(F32)
        tx_s[...] = total.astype(BF16)
        send(tx_s, tx_r, tx_sem, 0, x_mate())

    def update_gather():
        remote(tx_s, tx_r, tx_sem, 0, x_mate()).wait_recv()
        upd_v[zpos] = (tx_s[...].astype(F32) + tx_r[...].astype(F32)).astype(BF16)
        for d in range(1, 4):
            send(upd_v.at[zpos], upd_v.at[zpos], upd_sem, d, z_at(d))

    def update_end():
        for d in range(1, 4):
            slot = lax.rem(zpos + 4 - d, 4)
            remote(upd_v.at[slot], upd_v.at[slot], upd_sem, d, z_at(d)).wait_recv()
        for j in range(16):
            trail_v[j] = res_v[j] - upd_v[j // 4, j % 4].astype(F32)

    za(0)
    za(1)
    xs(1, ZP)
    step_begin()
    zd(1)
    zd(0)
    solve_pair(1)
    xs(0, ZM)
    update_first()
    z(1)
    xs(1, Z2)
    zc(0)
    solve_y(1)
    zc(1)
    xs(0, Z2)
    xs(0, ZP)
    solve_sum(1)
    update_scatter()
    xa(1)
    xs(1, ZM)
    xa(0)
    z(0)
    xd(1)
    xd(0)
    xs(1, Z0)
    update_swap()
    xc(0)
    xc(1)
    zx(0)
    xs(0, Z0)
    update_gather()
    zx(1)
    fx(1)
    fx(0)
    fz(1)
    fz(0)
    update_end()

    for copy in pending:
        copy.wait_send()
    for d in range(1, CHIPS):
        remote(l_s.at[0], l_r.at[d], l_sem, d, chip_at(d)).wait_send()


def store(trail_v, sol_v, out_v, trailing, solved, grm, sems):
    copies = [
        pltpu.make_async_copy(trail_v, trailing, sems.at[0]),
        pltpu.make_async_copy(sol_v, solved, sems.at[1]),
        pltpu.make_async_copy(out_v, grm, sems.at[2]),
    ]
    for copy in copies:
        copy.start()
    for copy in copies:
        copy.wait()


def shards(residual, diag_inverse, panels, first_block, probe_solved, genotypes, annotation):
    blocks, per_row, rhs = residual.shape
    rows = blocks * per_row
    snps = genotypes.shape[2]
    vmem = pltpu.VMEM
    sem = pltpu.SemaphoreType.DMA
    anywhere = pl.BlockSpec(memory_space=pl.ANY)
    in_vmem = pl.BlockSpec(memory_space=pltpu.VMEM)
    scratch = [
        vmem((16, 128, 128), F32), vmem((2, 256, 128), BF16), vmem((2, 16, 128, 256), BF16),
        vmem((rows, rhs), BF16), vmem((rhs, rows), BF16), vmem((rows, snps), BF16), vmem((16, 128), jnp.int32),
        vmem((2, 2, 128, 128), F32), vmem((2, 128, 128), F32), vmem((2, 128, 128), BF16), vmem((2, 128, 128), BF16),
        vmem((2, 4, 128, 128), BF16),
        vmem((2, 128, 128), F32), vmem((2, 128, 128), F32),
        vmem((128, 128), BF16), vmem((128, 128), BF16), vmem((4, 128, 128), BF16),
        vmem((16, 128, 128), F32), vmem((4, 4, 128, 128), BF16), vmem((4, 4, 128, 128), BF16),
        vmem((4, 128, 128), BF16), vmem((4, 128, 128), BF16), vmem((4, 4, 128, 128), BF16),
        vmem((4, 128, 256), BF16), vmem((4, 128, 256), BF16), vmem((4, 128, 256), F32),
        vmem((8, 128, 128), BF16), vmem((8, 128, 128), BF16),
        vmem((8, 128, 128), BF16), vmem((8, 128, 128), BF16), vmem((4, 256, snps), BF16),
        vmem((2, ZROWS, 256), BF16), vmem((2, ZROWS, 256), BF16), vmem((2, ZROWS, 256), BF16), vmem((2, ZROWS, 256), BF16),
        vmem((2, 2, ZROWS, 256), BF16), vmem((2, 4, XROWS, 128), BF16), vmem((2, 4, XROWS, 128), BF16),
        vmem((2, 4, XROWS, 128), F32), vmem((2, ZROWS, 256), F32), vmem((2, ZROWS, 128), BF16), vmem((2, ZROWS, 128), BF16),
        vmem((2, XROWS, 128), BF16), vmem((2, XROWS, 128), BF16), vmem((2, XROWS, 128), BF16), vmem((2, XROWS, 128), BF16),
        vmem((2, 2, XROWS, 128), BF16),
        pltpu.SMEM((1,), jnp.int32), sem((7,)), sem((8,)),
        sem((2, 2)), sem((2, 2)), sem((2, 8)), sem((2, 2)), sem((2, 1)), sem((2, 4)), sem((2, 4)), sem((2, 1)), sem((2, 4)),
        sem((2, 4)), sem((2, 8)), sem((2, 8)), sem((2, 8)), sem((2, 2)), sem((2, 4)), sem((2, 8)), sem((2, 2)),
        sem((2, 2)), sem((2, 4)),
    ]
    results = (
        jax.ShapeDtypeStruct((blocks, per_row, rhs), F32),
        jax.ShapeDtypeStruct((2, 2, 128, 128), F32),
        jax.ShapeDtypeStruct((rows, rhs), BF16),
    )
    parts = pl.pallas_call(
        kernel,
        out_shape=tuple(pltpu.VMEM(r.shape, r.dtype) for r in results),
        in_specs=[anywhere] * 7,
        out_specs=(in_vmem,) * 3,
        scratch_shapes=scratch,
        compiler_params=pltpu.CompilerParams(
            collective_id=0, has_side_effects=True, vmem_limit_bytes=58 * 1024 * 1024
        ),
        cost_estimate=pl.CostEstimate(flops=10_000_000_000, bytes_accessed=14_000_000, transcendentals=0),
    )(
        first_block, residual, diag_inverse, panels, probe_solved.reshape(rows, rhs),
        genotypes.reshape(rows, snps), annotation.reshape(16, 128),
    )
    trailing, solved, grm = pl.pallas_call(
        store,
        out_shape=results,
        in_specs=[anywhere] * 3,
        out_specs=(anywhere,) * 3,
        scratch_shapes=[sem((3,))],
        compiler_params=pltpu.CompilerParams(vmem_limit_bytes=4 * 1024 * 1024),
    )(*parts)
    return (
        trailing,
        solved.reshape(2, 256, 128),
        grm.reshape(blocks, per_row, 1, rhs),
    )


def solution(mesh):
    in_specs = (
        P(None, "row", None),
        P(None, "col", "row"),
        P(None, None, "row", "col"),
        P(),
        P(None, "row", None),
        P(None, "row", "col"),
        P("col"),
    )
    out_specs = (P(None, "row", None), P(None, "col", None), P(None, "row", "col", None))
    return jax.shard_map(shards, mesh=mesh, in_specs=in_specs, out_specs=out_specs, check_vma=False)
```

time: 71.9 us -> 68.8 us (0.957)
  Pallas kernels: 70.4 us -> 67.1 us
    pallas_call x1, Pallas kernels: 69.1 us -> 65.8 us  [shards(): pl.pallas_call(kernel, out_shape=tuple((pltpu.VMEM(r.shape, r.dtype) for...]
where the time goes in v3:
time: 68.8 us; the launch traced here: 68.5 us
  Pallas kernels  67.1 us (98%)
  between operations  1.45 us (2%)
    pallas_call x1, Pallas kernels, shards(): pl.pallas_call(kernel, out_shape=tuple((pltpu.VMEM(r.shape, r.dtype) for...  65.8 us

profile of v3, /device:TPU:0, one launch (start us, length us, event | category | flops | bytes accessed | tf_op | source)
XLA Modules:
  0.0 68.5 jit_solution(14392243100267315319)
XLA Ops:
  1.3 65.8 %shard_map.94 = (f32[16,128,128]{2,1,0:T(8,128)S(1)}, f32[2,2,128,128]{3,2,1,0:T(8,128)S(1)}, bf16[2048,128]{1,0:T(8,128)(2,1)S(1)}) custom-call(s32[1]{0:T(128)S(6)} %copy.11.first_ref, f32[16,128,128]{2,1,0:T(8,128)} %residual.1, bf16[2,256,128]{2,1,0:T(8,128)(2,1)} %diag.1, bf16[2,16,128,256]{3,2,1,0:T(8,128)(2,1)} %panels.1, bf16[2048,128]{1,0:T(8,128)(2,1)} %bitcast.8, ...), custom_call_target="tpu_custom_call" | custom-call | flops 10000000000 | bytes 14000000 | tf_op jit(solution)/shard_map/pallas_call | solution.py:418
  67.1 1.3 %shard_map.95 = (f32[16,128,128]{2,1,0:T(8,128)}, f32[2,2,128,128]{3,2,1,0:T(8,128)}, bf16[2048,128]{1,0:T(8,128)(2,1)}) custom-call(f32[16,128,128]{2,1,0:T(8,128)S(1)} %get-tuple-element.9.trail_v, f32[2,2,128,128]{3,2,1,0:T(8,128)S(1)} %get-tuple-element.10.sol_v, bf16[2048,128]{1,0:T(8,128)(2,1)S(1)} %get-tuple-element.11.out_v), custom_call_target="tpu_custom_call" | custom-call | tf_op jit(solution)/shard_map/pallas_call | solution.py:432

commit v4 on v3

--- a/solution.py
+++ b/solution.py
@@ -10,9 +10,10 @@
 BF16 = jnp.bfloat16
 SNPS = 16384
 CHIPS = 8
+FAR_FIRST = (6, 5, 7, 2, 4, 1, 3)
 COLS = 8
-ZROWS = 448
-XROWS = 576
+ZROWS = 528
+XROWS = 496
 
 
 def dot(a, b):
@@ -39,13 +40,19 @@
     row, col = lax.axis_index("row"), lax.axis_index("col")
     chip, core = lax.div(row, 2), lax.rem(row, 2)
     zpos, xhi = lax.div(col, 2), lax.rem(col, 2)
-    ypos = lax.rem(chip, 4)
+    xpos, ypos = lax.div(chip, 4), lax.rem(chip, 4)
 
     def mate():
         return (chip * 2 + (1 - core), col)
 
+    def chip_up(offset):
+        return lax.rem(xpos + offset // 4, 2) * 4 + lax.rem(ypos + offset % 4, 4)
+
+    def chip_down(offset):
+        return lax.rem(xpos + offset // 4, 2) * 4 + lax.rem(ypos + 4 - offset % 4, 4)
+
     def chip_at(offset):
-        return (lax.rem(chip + offset, CHIPS) * 2 + core, col)
+        return (chip_up(offset) * 2 + core, col)
 
     def y_at(offset):
         return ((lax.div(chip, 4) * 4 + lax.rem(ypos + offset, 4)) * 2 + core, col)
@@ -160,21 +167,17 @@
         remote(lo_s.at[g], lo_r.at[g], lo_sem, g, mate()).wait_recv()
         part = (lp_v[g] + lo_r[g].astype(F32)).astype(BF16)
         for h in range(2):
-            p = 2 * g + h
-            l_s[p] = part[:, h * 128:(h + 1) * 128]
-
-            @pl.when(chip != p)
-            def _():
-                d = lax.rem(p + CHIPS - chip, CHIPS)
-                remote(l_s.at[p], l_r.at[d], l_sem, d, (p * 2 + core, col)).start()
+            l_s[2 * g + h] = part[:, h * 128:(h + 1) * 128]
+    for d in FAR_FIRST:
+        send(l_s.at[chip_up(d)], l_r.at[d], l_sem, d, chip_at(d))
 
     solve_y(0)
     total = l_s[chip].astype(F32)
-    for d in range(1, CHIPS):
+    for d in reversed(FAR_FIRST):
         remote(l_s.at[0], l_r.at[d], l_sem, d, chip_at(d)).wait_recv()
         total = total + l_r[d].astype(F32)
     lf_v[chip] = (total * (1.0 / SNPS)).astype(BF16)
-    for d in range(1, CHIPS):
+    for d in FAR_FIRST:
         send(lf_v.at[chip], lf_v.at[chip], lf_sem, d, chip_at(d))
     send(lf_v.at[chip], lfo_v.at[chip], lfo_sem, 0, mate())
 
@@ -198,8 +201,8 @@
                 w_v[s, side * 128:(side + 1) * 128, lanes] = value * mask
 
     build(1, chip, lf_v[chip])
-    for d in range(1, CHIPS):
-        slot = lax.rem(chip + CHIPS - d, CHIPS)
+    for d in reversed(FAR_FIRST):
+        slot = chip_down(d)
         remote(lf_v.at[slot], lf_v.at[slot], lf_sem, d, chip_at(d)).wait_recv()
         send(lf_v.at[slot], lfo_v.at[slot], lfo_sem, d, mate())
         build(1, slot, lf_v[slot])
@@ -207,8 +210,8 @@
     u_r[zpos] = (u_s[...].astype(F32) + u_x[...].astype(F32)).astype(BF16)
     for d in range(1, 4):
         send(u_r.at[zpos], u_r.at[zpos], u_sem, d, z_at(d))
-    for d in range(CHIPS):
-        slot = lax.rem(chip + CHIPS - d, CHIPS)
+    for d in (0,) + FAR_FIRST[::-1]:
+        slot = chip_down(d)
         remote(lf_v.at[slot], lfo_v.at[slot], lfo_sem, d, mate()).wait_recv()
         build(0, slot, lfo_v[slot])
 
@@ -300,72 +303,88 @@
         for j in range(16):
             keep = jnp.where(j > block + 1, 1.0, 0.0).astype(F32)
             t_s[j // 4, j % 4] = (t0_v[j] + dot(pan_v[1, j], solved1) * keep).astype(BF16)
-        for d in range(1, 4):
-            send(t_s.at[lax.rem(zpos + d, 4)], t_r.at[d], t_sem, d, z_at(d))
+        far, up, down = (lax.rem(zpos + d, 4) for d in (2, 1, 3))
+        send(t_s.at[far, pl.ds(0, 2)], t_r.at[0, pl.ds(0, 2)], t_sem, 0, z_at(1))
+        send(t_s.at[far, pl.ds(2, 2)], t_r.at[0, pl.ds(2, 2)], t_sem, 1, z_at(3))
+        send(t_s.at[up, pl.ds(2, 2)], t_r.at[1, pl.ds(2, 2)], t_sem, 2, z_at(1))
+        send(t_s.at[down, pl.ds(0, 2)], t_r.at[2, pl.ds(0, 2)], t_sem, 3, z_at(3))
+
+    def update_relay():
+        for way, near, part in ((0, lax.rem(zpos + 1, 4), 0), (1, lax.rem(zpos + 3, 4), 2)):
+            rows = pl.ds(part, 2)
+            remote(t_s.at[near, rows], t_r.at[0, rows], t_sem, way, z_at(WAY[way])).wait_recv()
+            t_s[near, rows] = (t_s[near, rows].astype(F32) + t_r[0, rows].astype(F32)).astype(BF16)
+            send(t_s.at[near, rows], t_r.at[1 + way, rows], t_sem, 4 + way, z_at(WAY[way]))
 
     def update_swap():
-        total = t_s[zpos].astype(F32)
-        for d in range(1, 4):
-            remote(t_s.at[0], t_r.at[d], t_sem, d, z_at(d)).wait_recv()
-            total = total + t_r[d].astype(F32)
-        tx_s[...] = total.astype(BF16)
+        for way, early, late in ((0, 2, 0), (1, 0, 2)):
+            remote(t_s.at[0, pl.ds(early, 2)], t_r.at[1 + way, pl.ds(early, 2)], t_sem, 2 + way, z_at(WAY[way])).wait_recv()
+            remote(t_s.at[0, pl.ds(late, 2)], t_r.at[1 + way, pl.ds(late, 2)], t_sem, 4 + way, z_at(WAY[way])).wait_recv()
+        tx_s[...] = (t_s[zpos].astype(F32) + t_r[1].astype(F32) + t_r[2].astype(F32)).astype(BF16)
         send(tx_s, tx_r, tx_sem, 0, x_mate())
 
     def update_gather():
         remote(tx_s, tx_r, tx_sem, 0, x_mate()).wait_recv()
         upd_v[zpos] = (tx_s[...].astype(F32) + tx_r[...].astype(F32)).astype(BF16)
-        for d in range(1, 4):
-            send(upd_v.at[zpos], upd_v.at[zpos], upd_sem, d, z_at(d))
+        for way in range(2):
+            send(upd_v.at[zpos], upd_v.at[zpos], upd_sem, way, z_at(WAY[way]))
+
+    def update_pass():
+        for way, slot, part in ((0, lax.rem(zpos + 3, 4), 0), (1, lax.rem(zpos + 1, 4), 2)):
+            rows = pl.ds(part, 2)
+            remote(upd_v.at[slot], upd_v.at[slot], upd_sem, way, z_at(WAY[way])).wait_recv()
+            send(upd_v.at[slot, rows], upd_v.at[slot, rows], upd_sem, 2 + way, z_at(WAY[way]))
 
     def update_end():
-        for d in range(1, 4):
-            slot = lax.rem(zpos + 4 - d, 4)
-            remote(upd_v.at[slot], upd_v.at[slot], upd_sem, d, z_at(d)).wait_recv()
+        far = lax.rem(zpos + 2, 4)
+        for way, part in ((0, 0), (1, 2)):
+            rows = pl.ds(part, 2)
+            remote(upd_v.at[far, rows], upd_v.at[far, rows], upd_sem, 2 + way, z_at(WAY[way])).wait_recv()
         for j in range(16):
             trail_v[j] = res_v[j] - upd_v[j // 4, j % 4].astype(F32)
 
     za(0)
     za(1)
-    xs(1, ZP)
     step_begin()
+    update_first()
     zd(1)
-    zd(0)
     solve_pair(1)
     xs(0, ZM)
-    update_first()
-    z(1)
+    zd(0)
+    xs(1, ZP)
+    solve_y(1)
     xs(1, Z2)
-    zc(0)
-    solve_y(1)
-    zc(1)
+    solve_sum(1)
+    xs(1, ZM)
     xs(0, Z2)
-    xs(0, ZP)
-    solve_sum(1)
     update_scatter()
-    xa(1)
-    xs(1, ZM)
-    xa(0)
-    z(0)
     xd(1)
     xd(0)
     xs(1, Z0)
+    xs(0, ZP)
+    update_relay()
+    zc(1)
+    zc(0)
     update_swap()
+    xs(0, Z0)
+    z(1)
+    xa(0)
+    z(0)
+    xa(1)
+    update_gather()
+    zx(0)
+    xc(1)
+    zx(1)
     xc(0)
-    xc(1)
-    zx(0)
-    xs(0, Z0)
-    update_gather()
-    zx(1)
+    update_pass()
+    fz(1)
+    fz(0)
     fx(1)
     fx(0)
-    fz(1)
-    fz(0)
     update_end()
 
     for copy in pending:
         copy.wait_send()
-    for d in range(1, CHIPS):
-        remote(l_s.at[0], l_r.at[d], l_sem, d, chip_at(d)).wait_send()
 
 
 def store(trail_v, sol_v, out_v, trailing, solved, grm, sems):
@@ -406,7 +425,7 @@
         vmem((2, XROWS, 128), BF16), vmem((2, XROWS, 128), BF16), vmem((2, XROWS, 128), BF16), vmem((2, XROWS, 128), BF16),
         vmem((2, 2, XROWS, 128), BF16),
         pltpu.SMEM((1,), jnp.int32), sem((7,)), sem((8,)),
-        sem((2, 2)), sem((2, 2)), sem((2, 8)), sem((2, 2)), sem((2, 1)), sem((2, 4)), sem((2, 4)), sem((2, 1)), sem((2, 4)),
+        sem((2, 2)), sem((2, 2)), sem((2, 8)), sem((2, 2)), sem((2, 1)), sem((2, 4)), sem((2, 6)), sem((2, 1)), sem((2, 4)),
         sem((2, 4)), sem((2, 8)), sem((2, 8)), sem((2, 8)), sem((2, 2)), sem((2, 4)), sem((2, 8)), sem((2, 2)),
         sem((2, 2)), sem((2, 4)),
     ]

time: 68.8 us -> 68.4 us (level)
  no operation moved by 1% of the time
where the time goes in v4:
time: 68.4 us; the launch traced here: 68.2 us
  Pallas kernels  66.8 us (98%)
  between operations  1.45 us (2%)
    pallas_call x1, Pallas kernels, shards(): pl.pallas_call(kernel, out_shape=tuple((pltpu.VMEM(r.shape, r.dtype) for...  65.5 us

profile of v4, /device:TPU:0, one launch (start us, length us, event | category | flops | bytes accessed | tf_op | source)
XLA Modules:
  0.0 68.2 jit_solution(708523616856905030)
XLA Ops:
  1.3 65.5 %shard_map.94 = (f32[16,128,128]{2,1,0:T(8,128)S(1)}, f32[2,2,128,128]{3,2,1,0:T(8,128)S(1)}, bf16[2048,128]{1,0:T(8,128)(2,1)S(1)}) custom-call(s32[1]{0:T(128)S(6)} %copy.11.first_ref, f32[16,128,128]{2,1,0:T(8,128)} %residual.1, bf16[2,256,128]{2,1,0:T(8,128)(2,1)} %diag.1, bf16[2,16,128,256]{3,2,1,0:T(8,128)(2,1)} %panels.1, bf16[2048,128]{1,0:T(8,128)(2,1)} %bitcast.8, ...), custom_call_target="tpu_custom_call" | custom-call | flops 10000000000 | bytes 14000000 | tf_op jit(solution)/shard_map/pallas_call | solution.py:437
  66.8 1.3 %shard_map.95 = (f32[16,128,128]{2,1,0:T(8,128)}, f32[2,2,128,128]{3,2,1,0:T(8,128)}, bf16[2048,128]{1,0:T(8,128)(2,1)}) custom-call(f32[16,128,128]{2,1,0:T(8,128)S(1)} %get-tuple-element.9.trail_v, f32[2,2,128,128]{3,2,1,0:T(8,128)S(1)} %get-tuple-element.10.sol_v, bf16[2048,128]{1,0:T(8,128)(2,1)S(1)} %get-tuple-element.11.out_v), custom_call_target="tpu_custom_call" | custom-call | tf_op jit(solution)/shard_map/pallas_call | solution.py:451

commit v5 on v4

--- a/solution.py
+++ b/solution.py
@@ -82,7 +82,7 @@
         return copy
 
     barrier = pltpu.get_barrier_semaphore()
-    for d in range(1, CHIPS):
+    for d in FAR_FIRST:
         pl.semaphore_signal(barrier, inc=1, device_id=chip_at(d), device_id_type=MESH)
     for d in range(1, 4):
         pl.semaphore_signal(barrier, inc=1, device_id=z_at(d), device_id_type=MESH)
@@ -389,10 +389,11 @@
 
 def store(trail_v, sol_v, out_v, trailing, solved, grm, sems):
     copies = [
-        pltpu.make_async_copy(trail_v, trailing, sems.at[0]),
-        pltpu.make_async_copy(sol_v, solved, sems.at[1]),
-        pltpu.make_async_copy(out_v, grm, sems.at[2]),
-    ]
+        pltpu.make_async_copy(trail_v.at[pl.ds(4 * j, 4)], trailing.at[pl.ds(4 * j, 4)], sems.at[j]) for j in range(4)
+    ] + [
+        pltpu.make_async_copy(out_v.at[pl.ds(1024 * j, 1024)], grm.at[pl.ds(1024 * j, 1024)], sems.at[4 + j])
+        for j in range(2)
+    ] + [pltpu.make_async_copy(sol_v, solved, sems.at[6])]
     for copy in copies:
         copy.start()
     for copy in copies:
@@ -453,7 +454,7 @@
         out_shape=results,
         in_specs=[anywhere] * 3,
         out_specs=(anywhere,) * 3,
-        scratch_shapes=[sem((3,))],
+        scratch_shapes=[sem((7,))],
         compiler_params=pltpu.CompilerParams(vmem_limit_bytes=4 * 1024 * 1024),
     )(*parts)
     return (

time: 68.4 us -> 68.4 us (level)
  no operation moved by 1% of the time
where the time goes in v5:
time: 68.4 us; the launch traced here: 68.3 us
  Pallas kernels  66.8 us (98%)
  between operations  1.45 us (2%)
    pallas_call x1, Pallas kernels, shards(): pl.pallas_call(kernel, out_shape=tuple((pltpu.VMEM(r.shape, r.dtype) for...  65.5 us

profile of v5, /device:TPU:0, one launch (start us, length us, event | category | flops | bytes accessed | tf_op | source)
XLA Modules:
  0.0 68.3 jit_solution(12780544392815391860)
XLA Ops:
  1.3 65.5 %shard_map.94 = (f32[16,128,128]{2,1,0:T(8,128)S(1)}, f32[2,2,128,128]{3,2,1,0:T(8,128)S(1)}, bf16[2048,128]{1,0:T(8,128)(2,1)S(1)}) custom-call(s32[1]{0:T(128)S(6)} %copy.11.first_ref, f32[16,128,128]{2,1,0:T(8,128)} %residual.1, bf16[2,256,128]{2,1,0:T(8,128)(2,1)} %diag.1, bf16[2,16,128,256]{3,2,1,0:T(8,128)(2,1)} %panels.1, bf16[2048,128]{1,0:T(8,128)(2,1)} %bitcast.8, ...), custom_call_target="tpu_custom_call" | custom-call | flops 10000000000 | bytes 14000000 | tf_op jit(solution)/shard_map/pallas_call | solution.py:438
  66.8 1.3 %shard_map.95 = (f32[16,128,128]{2,1,0:T(8,128)}, f32[2,2,128,128]{3,2,1,0:T(8,128)}, bf16[2048,128]{1,0:T(8,128)(2,1)}) custom-call(f32[16,128,128]{2,1,0:T(8,128)S(1)} %get-tuple-element.9.trail_v, f32[2,2,128,128]{3,2,1,0:T(8,128)S(1)} %get-tuple-element.10.sol_v, bf16[2048,128]{1,0:T(8,128)(2,1)S(1)} %get-tuple-element.11.out_v), custom_call_target="tpu_custom_call" | custom-call | tf_op jit(solution)/shard_map/pallas_call | solution.py:452
